TPU v7x, 32 devices: a whole 2x2x4 slice. The times are simulated.
32 devices in a mesh: groups: 2 (over y), dp: 4 (over x, core), layer: 4 (over z).
Axes of the slice: x: 2, y: 2, z: 4, core: 2. Of those that a mesh axis runs over, the one named last changes fastest.
Arguments:
- train_grads: bfloat16 [8192, 4, 4096], P(('groups', 'dp'), 'layer'), parts along dimension 0, may hold values from -6 to 6
- query_grads: bfloat16 [512, 4, 4096], P('dp', 'layer'), may hold values from -6 to 6
- basis_out: float32 [4, 64, 64], P('layer'), may hold values from -0.75 to 0.75
- basis_in: float32 [4, 64, 64], P('layer'), may hold values from -0.75 to 0.75
- scaling: float32 [4, 64, 64], P('layer'), may hold values from 0.05 to 2
Outputs:
- scores: float32 [512, 8192], P('layer', ('groups', 'dp')), parts along dimension 1
There are 2 independent parts, one for each index of `groups`. A program takes and returns all parts, laid end to end along the dimension named above; an argument that names none is the same for every part. Nothing has to cross between parts.
All inputs are finite; a program needn't handle non-finite values.
Results may differ from a plain program's by a relative error of at most 0.0029.
Values may be sent and summed in bfloat16 or wider, within the bound.
A program may use at most 192 MiB of HBM per device.

v0:
```python
import jax
import jax.numpy as jnp
from jax import lax
from jax.sharding import PartitionSpec as P

damping = 0.1


def precondition(grads, out_basis, in_basis, corrected):
    count = grads.shape[0]
    matrix = grads.astype(jnp.float32).reshape(count, out_basis.shape[0], in_basis.shape[0])
    hp = lax.Precision.HIGHEST
    right = jnp.einsum("mcb,bd->mcd", matrix, in_basis, precision=hp)
    rotated = jnp.einsum("ca,mcd->mad", out_basis, right, precision=hp)
    damped = rotated / (corrected + damping)
    back = jnp.einsum("mad,ed->mae", damped, in_basis, precision=hp)
    result = jnp.einsum("ca,mae->mce", out_basis, back, precision=hp)
    return result.reshape(count, -1).astype(jnp.bfloat16)


def body(train_grads, query_grads, basis_out, basis_in, scaling):
    train_rows = train_grads[:, 0, :]
    local_queries = query_grads[:, 0, :]
    out_basis = basis_out[0]
    in_basis = basis_in[0]
    corrected = scaling[0]
    partial_scores = jnp.einsum(
        "mk,nk->mn",
        precondition(
            lax.all_gather(local_queries, "dp", axis=0, tiled=True), out_basis, in_basis, corrected
        ),
        train_rows,
        preferred_element_type=jnp.float32,
    )
    return lax.psum_scatter(partial_scores, "layer", scatter_dimension=0, tiled=True)


def solution(mesh):
    in_specs = (
        P(("groups", "dp"), "layer", None),
        P("dp", "layer", None),
        P("layer", None, None),
        P("layer", None, None),
        P("layer", None, None),
    )
    out_specs = P("layer", ("groups", "dp"))
    return jax.shard_map(body, mesh=mesh, in_specs=in_specs, out_specs=out_specs, check_vma=False)
```

profile of v0, /device:TPU:0, one launch (start us, length us, event | category | flops | bytes accessed | tf_op | source)
XLA Modules:
  0.0 154.4 jit_solution(15633172028491800944)
XLA Ops:
  6.5 0.0 copy-start
  6.5 0.0 copy-start.1
  6.5 0.0 all-gather.3.cloned.1.call-start
  6.5 2.3 %copy.18 = bf16[128,1,4096]{0,2,1:T(8,128)(2,1)} copy(bf16[128,1,4096]{2,0,1:T(8,128)(2,1)} %param.6) | data formatting | bytes 2097152 | tf_op args[1]
  8.8 0.0 all-gather.3.cloned.1.call-update
  8.9 0.0 reduce-scatter.2.cloned.1.call-start
  8.9 0.8 add_bitcast_fusion
  9.7 0.1 copy.22
  9.7 37.0 %all-gather.3.cloned.1.call-done = bf16[512,1,4096]{0,2,1:T(8,128)(2,1)} async-done(((bf16[128,1,4096]{0,2,1:T(8,128)(2,1)}), bf16[512,1,4096]{0,2,1:T(8,128)(2,1)}) %all-gather.3.cloned.1.call-update) | async-done | bytes 4194320 | tf_op jit(solution)/shard_map/all_gather | solution.py:30
  46.8 0.0 copy-done
  46.8 6.5 %fusion.15 = f32[512,64,64]{0,2,1:T(8,128)S(1)} fusion(bf16[512,64,64]{0,2,1:T(8,128)(2,1)} %bitcast.29, f32[1,64,64]{2,1,0:T(8,128)S(1)} %copy-done), kind=kOutput, calls=%fused_computation.13 | convolution fusion | flops 1610612736 | bytes 12599296 | tf_op jit(solution)/shard_map/mcb,bd->mcd/dot_general | solution.py:13
  53.3 0.0 copy-done.1
  53.3 15.6 %bitcast_divide_fusion = f32[512,64,64]{0,1,2:T(8,128)S(1)} fusion(f32[64,64]{0,1:T(8,128)S(1)} %copy.22, f32[512,64,64]{0,2,1:T(8,128)S(1)} %fusion.15, f32[1,64,64]{2,1,0:T(8,128)S(1)} %copy-done.1), kind=kOutput, calls=%fused_computation.2 | convolution fusion | flops 1612709888 | bytes 16809984 | tf_op jit(solution)/shard_map/ca,mcd->mad/dot_general | solution.py:14
  69.0 0.0 slice-start
  69.0 14.8 %fusion.4 = f32[512,64,64]{0,2,1:T(8,128)S(1)} fusion(f32[512,64,64]{0,1,2:T(8,128)S(1)} %bitcast_divide_fusion, f32[1,64,64]{2,1,0:T(8,128)S(1)} %copy-done), kind=kOutput, calls=%fused_computation.5 | convolution fusion | flops 1610612736 | bytes 16793600 | tf_op jit(solution)/shard_map/mad,ed->mae/dot_general | solution.py:16
  83.8 0.0 slice-start.1
  83.8 11.2 %convert_bitcast_fusion = bf16[512,64,64]{0,1,2:T(8,128)(2,1)S(1)} fusion(f32[512,64,64]{0,2,1:T(8,128)S(1)} %fusion.4, f32[1,64,64]{2,1,0:T(8,128)S(1)} %copy-done.1), kind=kOutput, calls=%fused_computation.9 | convolution fusion | flops 1612709888 | bytes 12599296 | tf_op jit(solution)/shard_map/ca,mae->mce/dot_general | solution.py:17
  95.0 2.4 %copy.25 = bf16[512,64,64]{0,2,1:T(8,128)(2,1)S(1)} copy(bf16[512,64,64]{0,1,2:T(8,128)(2,1)S(1)} %convert_bitcast_fusion) | data formatting | bytes 8388608 | tf_op jit(solution)/shard_map/convert_element_type | solution.py:18
  97.3 0.0 slice-done
  97.4 0.0 slice-done.1
  97.4 5.9 %fusion = f32[512,1024]{1,0:T(8,128)} fusion(bf16[512,4096]{0,1:T(8,128)(2,1)S(1)} %bitcast.30, bf16[1024,1,4096]{2,0,1:T(8,128)(2,1)S(1)} %bitcast.32), kind=kOutput, calls=%fused_computation | convolution fusion | flops 4294967296 | bytes 14680064 | tf_op jit(solution)/shard_map/mk,nk->mn/dot_general | solution.py:27
  103.3 0.0 reduce-scatter.2.cloned.1.call-update
  103.3 44.0 %reduce-scatter.2.cloned.1.call-done = f32[128,1024]{1,0:T(8,128)} async-done(((f32[512,1024]{1,0:T(8,128)}), f32[128,1024]{1,0:T(8,128)}) %reduce-scatter.2.cloned.1.call-update) | async-done | bytes 524304 | tf_op jit(solution)/shard_map/reduce_scatter | solution.py:35
  (1 shorter events, 0.0 us)
Async XLA Ops:
  6.5 40.2 %copy-start = (f32[1,64,64]{2,1,0:T(8,128)S(1)}, f32[1,64,64]{2,1,0:T(8,128)}, u32[]{:S(2)}) copy-start(f32[1,64,64]{2,1,0:T(8,128)} %param.8) | copy-start | bytes 49156
  6.5 46.8 %copy-start.1 = (f32[1,64,64]{2,1,0:T(8,128)S(1)}, f32[1,64,64]{2,1,0:T(8,128)}, u32[]{:S(2)}) copy-start(f32[1,64,64]{2,1,0:T(8,128)} %param.7) | copy-start | bytes 49156
  6.5 40.2 %all-gather.3.cloned.1.call-start = ((), (), s32[]{:S(2)}) async-start(), calls=%async_computation.2 | async-start | bytes 5242880 | tf_op jit(solution)/shard_map/all_gather | solution.py:30
  8.9 138.5 %reduce-scatter.2.cloned.1.call-start = ((), (), s32[]{:S(2)}) async-start(), calls=%async_computation.1 | async-start | bytes 2621440 | tf_op jit(solution)/shard_map/reduce_scatter | solution.py:35
  69.0 28.4 %slice-start = ((s8[8388608]{0:T(1024)(128)(4,1)}), s8[4194304]{0:T(1024)(128)(4,1)S(1)}, s32[]{:S(2)}) async-start(s8[8388608]{0:T(1024)(128)(4,1)} %bitcast.31), calls=%async_computation.3 | async-start | bytes 8388608
  83.8 13.6 %slice-start.1 = ((s8[8388608]{0:T(1024)(128)(4,1)}), s8[4194304]{0:T(1024)(128)(4,1)S(1)}, s32[]{:S(2)}) async-start(s8[8388608]{0:T(1024)(128)(4,1)} %bitcast.31), calls=%async_computation.4 | async-start | bytes 8388608
Sparse Core Ops, SparseCore 0:
  9.0 37.7 all-gather.2
  103.4 43.8 reduce-scatter.1
where the time goes:
time: 157 us; the launch traced here: 154 us
  waiting for transfers between devices  81.1 us (52%)
  matrix products  54 us (34%)
  between operations  13.8 us (9%)
  local copies, waits for them, and re-layouts  4.76 us (3%)
    reduce_scatter x1, waiting for transfers between devices, body(): lax.psum_scatter(partial_scores, 'layer', scatter_dimension=0, tiled=True)  44 us
    all_gather x1, waiting for transfers between devices, body(): lax.all_gather(local_queries, 'dp', axis=0, tiled=True)  37 us
    dot_general x1, matrix products, precondition(): rotated = jnp.einsum('ca,mcd->mad', out_basis, right, precision=hp)  15.6 us
    dot_general x1, matrix products, precondition(): back = jnp.einsum('mad,ed->mae', damped, in_basis, precision=hp)  14.8 us
    dot_general x1, matrix products, precondition(): result = jnp.einsum('ca,mae->mce', out_basis, back, precision=hp)  11.2 us
    dot_general x1, matrix products, precondition(): right = jnp.einsum('mcb,bd->mcd', matrix, in_basis, precision=hp)  6.53 us
    dot_general x1, matrix products, body(): jnp.einsum('mk,nk->mn', precondition(lax.all_gather(local_queries, 'dp',...  5.89 us
  transfers between devices with their start and end apart: 2, of which 2 were waited for; matrix products, arithmetic and copies ran while one was open for 1% of the time, Pallas kernels for 0%

commit v1 on v0

v1 whole, which is shorter than its diff:
```python
import functools

import jax
import jax.numpy as jnp
from jax import lax
from jax.experimental import pallas as pl
from jax.experimental.pallas import tpu as pltpu
from jax.sharding import PartitionSpec as P

damping = 0.1
f32 = jnp.float32
bf16 = jnp.bfloat16
MESH = pl.DeviceIdType.MESH
VMEM_LIMIT = 56 * 1024 * 1024
NT = (((1,), (1,)), ((), ()))
D = 64
CHUNK = 16


def dot_nt(a, b):
    return lax.dot_general(a, b, NT, preferred_element_type=f32)


def high_low(x):
    high = x.astype(bf16)
    return high, (x - high.astype(f32)).astype(bf16)


def lane_split(x):
    high, low = high_low(x)
    lane = lax.broadcasted_iota(jnp.int32, x.shape, 1)
    return jnp.where((lane // D) % 2 == 0, high.astype(f32), low.astype(f32)).astype(bf16)


def row_split(x):
    high, low = high_low(x)
    return jnp.concatenate([high, high, low, low], axis=0)


def precondition_kernel(
    g_ref, bo_ref, bi_ref, s_ref, p_ref, wide, tall, square, rot, back, bo4, bi4, d4, w_in
):
    count = g_ref.shape[0]
    bo, bi = bo_ref[...], bi_ref[...]
    inverse = 1.0 / (s_ref[...] + damping)

    for j in range(4):
        bo4[:, j * D : (j + 1) * D] = bo
        bi4[:, j * D : (j + 1) * D] = bi
        for i in range(4):
            wide[i * D : (i + 1) * D, j * D : (j + 1) * D] = bo
    lane = lax.broadcasted_iota(jnp.int32, wide.shape, 1)
    high, low = high_low(wide[...])
    wide_split = jnp.where(lane < 2 * D, high.astype(f32), low.astype(f32)).astype(bf16)
    tall[...] = jnp.zeros_like(tall)
    for j in range(4):
        tall[j * D : (j + 1) * D, 0:D] = inverse
    d4[...] = jnp.transpose(tall[...])
    square[...] = jnp.zeros_like(square)
    square[0:D, 0:D] = bi
    square[D : 2 * D, D : 2 * D] = bi
    high, low = high_low(jnp.transpose(square[...]))
    w_in[...] = jnp.concatenate([high, low], axis=1)
    bi4_split = lane_split(bi4[...])

    weights = w_in[...]
    for pair in range(D // 2):
        block = g_ref[:, pair * 2 * D : (pair + 1) * 2 * D]
        rot[pair * 2 * D : (pair + 1) * 2 * D, :] = dot_nt(
            weights, jnp.concatenate([block, block], axis=1)
        )

    bo_four = bo4[...]
    group = 8

    def middle(step, carry):
        first = step * group
        scales = d4[pl.ds(pl.multiple_of(first, group), group), :]
        left = jnp.concatenate(
            [lane_split(bo_four * scales[i : i + 1, :]) for i in range(group)], axis=0
        )
        mats = lane_split(dot_nt(left, wide_split))
        for i in range(group):
            column = rot[pl.ds(first + i, D, stride=D), :]
            back[pl.ds(pl.multiple_of((first + i) * D, D), D), :] = jnp.dot(
                mats[i * D : (i + 1) * D, :], row_split(column), preferred_element_type=f32
            )
        return carry

    lax.fori_loop(0, D // group, middle, 0)

    for pair in range(D // 2):
        halves = [
            jnp.dot(
                bi4_split,
                row_split(back[pl.ds(2 * pair + i, D, stride=D), :]),
                preferred_element_type=f32,
            )
            for i in range(2)
        ]
        block = jnp.transpose(jnp.concatenate(halves, axis=0))
        p_ref[:, pair * 2 * D : (pair + 1) * 2 * D] = block.astype(bf16)


def precondition(grads, bo, bi, s):
    count, entries = grads.shape
    vmem = pl.BlockSpec(memory_space=pltpu.VMEM)
    return pl.pallas_call(
        precondition_kernel,
        out_shape=jax.ShapeDtypeStruct((count, entries), bf16),
        in_specs=[vmem] * 4,
        out_specs=vmem,
        scratch_shapes=[
            pltpu.VMEM((4 * D, 4 * D), f32),
            pltpu.VMEM((4 * D, 2 * D), f32),
            pltpu.VMEM((2 * D, 2 * D), f32),
            pltpu.VMEM((entries, count), f32),
            pltpu.VMEM((entries, count), f32),
            pltpu.VMEM((D, 4 * D), f32),
            pltpu.VMEM((D, 4 * D), f32),
            pltpu.VMEM((2 * D, 4 * D), f32),
            pltpu.VMEM((2 * D, 4 * D), bf16),
        ],
        compiler_params=pltpu.CompilerParams(vmem_limit_bytes=VMEM_LIMIT),
        name="precondition",
    )(grads, bo, bi, s)


def score_kernel(
    sizes,
    train_hbm,
    p_ref,
    out_ref,
    train,
    every,
    ours,
    theirs,
    train_sem,
    far_send,
    far_recv,
    row_send,
    row_recv,
    core_send,
    core_recv,
    sum_send,
    sum_recv,
):
    dp, layers = sizes
    chips = dp // 2
    per = dp // layers
    half = p_ref.shape[0] // 2
    chunks = half // CHUNK
    n = train.shape[0]
    y = lax.axis_index("groups")
    me = lax.axis_index("dp")
    z = lax.axis_index("layer")
    x, core = me // 2, me % 2

    load = pltpu.make_async_copy(train_hbm, train, train_sem)
    load.start()

    sibling = (y, 2 * x + 1 - core, z)
    across = (1 - y, me, z)
    far = [(y, 2 * ((x + o) % chips) + core, z) for o in range(1, chips)]
    owners = [(y, me, (z + o) % layers) for o in range(1, layers)]

    barrier = pltpu.get_barrier_semaphore()
    others = [sibling, across] + far + owners
    for other in others:
        pl.semaphore_signal(barrier, inc=1, device_id=other, device_id_type=MESH)
    pl.semaphore_wait(barrier, len(others))

    def rows(chunk):
        return pl.ds(chunk * CHUNK, CHUNK)

    started = []
    for chunk in range(chunks):
        for o in range(1, chips):
            source = p_ref.at[
                pl.ds(pl.multiple_of(y * half + chunk * CHUNK, CHUNK), CHUNK), :
            ]
            started.append(
                pltpu.make_async_remote_copy(
                    source,
                    every.at[x, y, core, rows(chunk), :],
                    far_send.at[o, chunk],
                    far_recv.at[o, chunk],
                    device_id=far[o - 1],
                    device_id_type=MESH,
                )
            )
            started[-1].start()
    for h in range(2):
        copy = pltpu.make_async_remote_copy(
            p_ref.at[pl.ds(h * half, half), :],
            every.at[x, h, core],
            core_send.at[0, h, 0],
            core_recv.at[0, h, 0],
            device_id=sibling,
            device_id_type=MESH,
        )
        copy.start()
        started.append(copy)
    for h in range(2):
        every[x, h, core] = p_ref[pl.ds(h * half, half), :]

    def arrived(ref, sem):
        pltpu.make_async_remote_copy(
            ref, ref, sem, sem, device_id=sibling, device_id_type=MESH
        ).wait_recv()

    def forward(chip, h, chunk, send, recv, to):
        block = every.at[chip, h, core, rows(chunk), :]
        copy = pltpu.make_async_remote_copy(
            block, block, send, recv, device_id=to, device_id_type=MESH
        )
        copy.start()
        started.append(copy)

    def unit_sum_copy(chip, h, c):
        block = 2 * chip + c
        place = block % per
        return block // per, place, lambda source: pltpu.make_async_remote_copy(
            ours.at[chip, h, c],
            theirs.at[source, place, h],
            sum_send.at[chip, h, c],
            sum_recv.at[source, place, h],
            device_id=(y, me, block // per),
            device_id_type=MESH,
        )

    tile = min(n, 256)

    def score(chip, hs):
        if len(hs) == 2:
            left_ref = every.at[chip]
        else:
            left_ref = every.at[chip, hs[0]]

        def step(t, carry):
            columns = pl.ds(pl.multiple_of(t * tile, tile), tile)
            left = left_ref[...].reshape(-1, every.shape[-1])
            product = dot_nt(left, train[columns, :])
            for i, h in enumerate(hs):
                for c in range(2):
                    block = 2 * chip + c
                    first = (i * 2 + c) * half
                    piece = product[first : first + half, :]
                    mine = block // per == z

                    @pl.when(mine)
                    def _():
                        start = pl.multiple_of((block % per) * 2 * half + h * half, half)
                        out_ref[pl.ds(start, half), columns] = piece

                    @pl.when(jnp.logical_not(mine))
                    def _():
                        ours[chip, h, c, :, columns] = piece.astype(bf16)

            return carry

        lax.fori_loop(0, n // tile, step, 0)
        for h in hs:
            for c in range(2):
                owner, _, copy = unit_sum_copy(chip, h, c)

                @pl.when(owner != z)
                def _():
                    copy(z).start()

    for h in range(2):
        arrived(every.at[x, h, 1 - core], core_recv.at[0, h, 0])
    load.wait()
    score(x, (0, 1))

    for o in range(1, chips):
        source = (x + chips - o) % chips
        for chunk in range(chunks):
            arrived(every.at[source, y, core, rows(chunk), :], far_recv.at[o, chunk])
            forward(source, y, chunk, row_send.at[o, chunk], row_recv.at[o, chunk], across)
            forward(
                source, y, chunk, core_send.at[o, 0, chunk], core_recv.at[o, 0, chunk], sibling
            )
        for chunk in range(chunks):
            arrived(every.at[source, y, 1 - core, rows(chunk), :], core_recv.at[o, 0, chunk])
        score(source, (y,))
    for o in range(1, chips):
        source = (x + chips - o) % chips
        for chunk in range(chunks):
            arrived(every.at[source, 1 - y, core, rows(chunk), :], row_recv.at[o, chunk])
            forward(
                source,
                1 - y,
                chunk,
                core_send.at[o, 1, chunk],
                core_recv.at[o, 1, chunk],
                sibling,
            )
        for chunk in range(chunks):
            arrived(
                every.at[source, 1 - y, 1 - core, rows(chunk), :], core_recv.at[o, 1, chunk]
            )
        score(source, (1 - y,))

    for place in range(per):
        for h in range(2):
            for o in range(1, layers):
                source = (z + o) % layers
                arrived(theirs.at[source, place, h], sum_recv.at[source, place, h])
            start = (place * 2 + h) * half
            total = out_ref[start : start + half, :]
            for o in range(1, layers):
                total = total + theirs[(z + o) % layers, place, h].astype(f32)
            out_ref[start : start + half, :] = total

    for copy in started:
        copy.wait_send()
    for chip in range(chips):
        for h in range(2):
            for c in range(2):
                if True:
                    owner, _, copy = unit_sum_copy(chip, h, c)

                    @pl.when(owner != z)
                    def _():
                        copy(z).wait_send()


def scores(train_rows, ready, dp, layers):
    n, entries = train_rows.shape
    count = ready.shape[0]
    chips, per, half = dp // 2, dp // layers, count // 2
    chunks = half // CHUNK
    vmem = pl.BlockSpec(memory_space=pltpu.VMEM)
    dma = pltpu.SemaphoreType.DMA
    return pl.pallas_call(
        functools.partial(score_kernel, (dp, layers)),
        out_shape=jax.ShapeDtypeStruct((per * count, n), f32),
        in_specs=[pl.BlockSpec(memory_space=pl.ANY), vmem],
        out_specs=vmem,
        scratch_shapes=[
            pltpu.VMEM((n, entries), bf16),
            pltpu.VMEM((chips, 2, 2, half, entries), bf16),
            pltpu.VMEM((chips, 2, 2, half, n), bf16),
            pltpu.VMEM((layers, per, 2, half, n), bf16),
            dma,
            dma((chips, chunks)),
            dma((chips, chunks)),
            dma((chips, chunks)),
            dma((chips, chunks)),
            dma((chips, 2, chunks)),
            dma((chips, 2, chunks)),
            dma((chips, 2, 2)),
            dma((layers, per, 2)),
        ],
        compiler_params=pltpu.CompilerParams(
            collective_id=0, has_side_effects=True, vmem_limit_bytes=VMEM_LIMIT
        ),
        name="scores",
    )(train_rows, ready)


def solution(mesh):
    dp, layers = mesh.shape["dp"], mesh.shape["layer"]

    def body(train_grads, query_grads, basis_out, basis_in, scaling):
        ready = precondition(query_grads[:, 0, :], basis_out[0], basis_in[0], scaling[0])
        return scores(train_grads[:, 0, :], ready, dp, layers)

    in_specs = (
        P(("groups", "dp"), "layer", None),
        P("dp", "layer", None),
        P("layer", None, None),
        P("layer", None, None),
        P("layer", None, None),
    )
    out_specs = P("layer", ("groups", "dp"))
    return jax.shard_map(body, mesh=mesh, in_specs=in_specs, out_specs=out_specs, check_vma=False)
```

time: 157 us -> 57.4 us (0.37)
  the two profiles are of different devices: /device:TPU:0 before, /device:TPU:29 now
where the time goes in v1:
time: 57.4 us; the launch traced here: 57.2 us
  Pallas kernels  55.3 us (96%)
  local copies, waits for them, and re-layouts  1.89 us (3%)
    pallas_call x1, Pallas kernels, scores(): pl.pallas_call(functools.partial(score_kernel, (dp, layers)), out_shape=j...  46.4 us
    pallas_call x1, Pallas kernels, precondition(): pl.pallas_call(precondition_kernel, out_shape=jax.ShapeDtypeStruct((count...  8.87 us
    unnamed x1, local copies, waits for them, and re-layouts  1.89 us

profile of v1, /device:TPU:29, one launch (start us, length us, event | category | flops | bytes accessed | tf_op | source)
XLA Modules:
  0.0 57.2 jit_solution(1616696931173698680)
XLA Ops:
  0.0 8.9 %precondition.1.p_ref = bf16[128,4096]{1,0:T(8,128)(2,1)} custom-call(bf16[128,4096]{1,0:T(8,128)(2,1)} %bitcast.6, f32[64,64]{1,0:T(8,128)} %bitcast.7, f32[64,64]{1,0:T(8,128)} %bitcast.8, f32[64,64]{1,0:T(8,128)} %bitcast.9), custom_call_target="tpu_custom_call" | custom-call | tf_op jit(solution)/shard_map/precondition/pallas_call | solution.py:108
  8.9 46.4 %scores.1 = f32[128,1024]{1,0:T(8,128)} custom-call(bf16[1024,4096]{1,0:T(8,128)(2,1)} %bitcast.5, bf16[128,4096]{1,0:T(8,128)(2,1)} %precondition.1.p_ref), custom_call_target="tpu_custom_call" | custom-call | tf_op jit(solution)/shard_map/scores/pallas_call | solution.py:336
  55.3 1.9 %copy.7 = f32[128,1024]{1,0:T(8,128)} copy(f32[128,1024]{1,0:T(8,128)} %scores.1) | data formatting | bytes 1048576

commit v2 on v1

--- a/solution.py
+++ b/solution.py
@@ -133,7 +133,9 @@
     out_ref,
     train,
     every,
+    exact,
     ours,
+    relay,
     theirs,
     train_sem,
     far_send,
@@ -144,6 +146,7 @@
     core_recv,
     sum_send,
     sum_recv,
+    relay_recv,
 ):
     dp, layers = sizes
     chips = dp // 2
@@ -217,73 +220,109 @@
         copy.start()
         started.append(copy)
 
-    def unit_sum_copy(chip, h, c):
+    partner = z + 1 - 2 * (z % 2)
+
+    def route(chip, h, c):
         block = 2 * chip + c
-        place = block % per
-        return block // per, place, lambda source: pltpu.make_async_remote_copy(
+        owner, place = block // per, block % per
+        inside = owner // 2 == z // 2
+        upward = owner > z
+        near = jnp.logical_not(inside) & (upward == (z % 2 == 1))
+        direct = inside & (owner != z)
+        outer = jnp.logical_not(inside) & (upward != (z % 2 == 1))
+        return owner, place, direct, outer, near
+
+    def sum_copy(chip, h, c):
+        owner, place, _, _, _ = route(chip, h, c)
+        return pltpu.make_async_remote_copy(
             ours.at[chip, h, c],
-            theirs.at[source, place, h],
+            theirs.at[z // 2, place, h],
             sum_send.at[chip, h, c],
-            sum_recv.at[source, place, h],
-            device_id=(y, me, block // per),
+            sum_recv.at[z // 2, place, h],
+            device_id=(y, me, owner),
             device_id_type=MESH,
         )
 
-    tile = min(n, 256)
-
-    def score(chip, hs):
-        if len(hs) == 2:
-            left_ref = every.at[chip]
-        else:
-            left_ref = every.at[chip, hs[0]]
-
-        def step(t, carry):
-            columns = pl.ds(pl.multiple_of(t * tile, tile), tile)
-            left = left_ref[...].reshape(-1, every.shape[-1])
-            product = dot_nt(left, train[columns, :])
-            for i, h in enumerate(hs):
-                for c in range(2):
-                    block = 2 * chip + c
-                    first = (i * 2 + c) * half
-                    piece = product[first : first + half, :]
-                    mine = block // per == z
-
-                    @pl.when(mine)
-                    def _():
-                        start = pl.multiple_of((block % per) * 2 * half + h * half, half)
-                        out_ref[pl.ds(start, half), columns] = piece
-
-                    @pl.when(jnp.logical_not(mine))
-                    def _():
-                        ours[chip, h, c, :, columns] = piece.astype(bf16)
-
-            return carry
-
-        lax.fori_loop(0, n // tile, step, 0)
+    def relay_copy(chip, h, c):
+        return pltpu.make_async_remote_copy(
+            ours.at[chip, h, c],
+            relay.at[chip, h, c],
+            sum_send.at[chip, h, c],
+            relay_recv.at[chip, h, c],
+            device_id=(y, me, partner),
+            device_id_type=MESH,
+        )
+
+    def send_sums(chip, hs):
         for h in hs:
             for c in range(2):
-                owner, _, copy = unit_sum_copy(chip, h, c)
-
-                @pl.when(owner != z)
+                _, _, direct, outer, _ = route(chip, h, c)
+
+                @pl.when(outer)
                 def _():
-                    copy(z).start()
+                    relay_copy(chip, h, c).start()
+
+                @pl.when(direct)
+                def _():
+                    sum_copy(chip, h, c).start()
+
+    def combine(chip, h, c):
+        _, _, _, _, near = route(chip, h, c)
+
+        @pl.when(near)
+        def _():
+            relay_copy(chip, h, c).wait_recv()
+            ours[chip, h, c] = (exact[chip, h, c] + relay[chip, h, c].astype(f32)).astype(bf16)
+            sum_copy(chip, h, c).start()
+
+    tile = min(n, 256)
+
+    def score_tile(chip, hs, t):
+        columns = pl.ds(pl.multiple_of(t * tile, tile), tile)
+        left = every[chip] if len(hs) == 2 else every[chip, hs[0]]
+        product = dot_nt(left.reshape(-1, every.shape[-1]), train[columns, :])
+        for i, h in enumerate(hs):
+            for c in range(2):
+                first = (i * 2 + c) * half
+                piece = product[first : first + half, :]
+                exact[chip, h, c, :, columns] = piece
+                ours[chip, h, c, :, columns] = piece.astype(bf16)
+
+    def score(chip, hs):
+        def step(t, carry):
+            score_tile(chip, hs, t)
+            return carry
+
+        lax.fori_loop(0, n // tile, step, 0)
+        send_sums(chip, hs)
 
     for h in range(2):
         arrived(every.at[x, h, 1 - core], core_recv.at[0, h, 0])
     load.wait()
-    score(x, (0, 1))
-
-    for o in range(1, chips):
-        source = (x + chips - o) % chips
-        for chunk in range(chunks):
+    def pass_on(chunk):
+        for o in range(1, chips):
+            source = (x + chips - o) % chips
             arrived(every.at[source, y, core, rows(chunk), :], far_recv.at[o, chunk])
             forward(source, y, chunk, row_send.at[o, chunk], row_recv.at[o, chunk], across)
             forward(
                 source, y, chunk, core_send.at[o, 0, chunk], core_recv.at[o, 0, chunk], sibling
             )
+
+    passed = 0
+    for t in range(n // tile):
+        score_tile(x, (0, 1), t)
+        if passed < chunks and t < n // tile - 1:
+            pass_on(passed)
+            passed += 1
+    send_sums(x, (0, 1))
+    for chunk in range(passed, chunks):
+        pass_on(chunk)
+    for o in range(1, chips):
+        source = (x + chips - o) % chips
         for chunk in range(chunks):
             arrived(every.at[source, y, 1 - core, rows(chunk), :], core_recv.at[o, 0, chunk])
         score(source, (y,))
+    pieces = [(h, c) for h in range(2) for c in range(2)]
     for o in range(1, chips):
         source = (x + chips - o) % chips
         for chunk in range(chunks):
@@ -296,34 +335,44 @@
                 core_recv.at[o, 1, chunk],
                 sibling,
             )
+            if o == 1 and chunk < len(pieces):
+                combine(x, *pieces[chunk])
+        if o == 1:
+            for h, c in pieces[chunks:]:
+                combine(x, h, c)
         for chunk in range(chunks):
             arrived(
                 every.at[source, 1 - y, 1 - core, rows(chunk), :], core_recv.at[o, 1, chunk]
             )
         score(source, (1 - y,))
-
+    for o in range(1, chips):
+        source = (x + chips - o) % chips
+        for h in (y, 1 - y):
+            for c in range(2):
+                combine(source, h, c)
+
+    pairs = layers // 2
     for place in range(per):
+        block = z * per + place
         for h in range(2):
-            for o in range(1, layers):
-                source = (z + o) % layers
+            for o in range(pairs):
+                source = (z // 2 + o) % pairs
                 arrived(theirs.at[source, place, h], sum_recv.at[source, place, h])
+            total = exact[block // 2, h, block % 2]
+            for o in range(pairs):
+                total = total + theirs[(z // 2 + o) % pairs, place, h].astype(f32)
             start = (place * 2 + h) * half
-            total = out_ref[start : start + half, :]
-            for o in range(1, layers):
-                total = total + theirs[(z + o) % layers, place, h].astype(f32)
             out_ref[start : start + half, :] = total
 
     for copy in started:
         copy.wait_send()
     for chip in range(chips):
-        for h in range(2):
-            for c in range(2):
-                if True:
-                    owner, _, copy = unit_sum_copy(chip, h, c)
-
-                    @pl.when(owner != z)
-                    def _():
-                        copy(z).wait_send()
+        for h, c in pieces:
+            owner, _, _, _, _ = route(chip, h, c)
+
+            @pl.when(owner != z)
+            def _():
+                relay_copy(chip, h, c).wait_send()
 
 
 def scores(train_rows, ready, dp, layers):
@@ -341,8 +390,10 @@
         scratch_shapes=[
             pltpu.VMEM((n, entries), bf16),
             pltpu.VMEM((chips, 2, 2, half, entries), bf16),
+            pltpu.VMEM((chips, 2, 2, half, n), f32),
             pltpu.VMEM((chips, 2, 2, half, n), bf16),
-            pltpu.VMEM((layers, per, 2, half, n), bf16),
+            pltpu.VMEM((chips, 2, 2, half, n), bf16),
+            pltpu.VMEM((layers // 2, per, 2, half, n), bf16),
             dma,
             dma((chips, chunks)),
             dma((chips, chunks)),
@@ -351,7 +402,8 @@
             dma((chips, 2, chunks)),
             dma((chips, 2, chunks)),
             dma((chips, 2, 2)),
-            dma((layers, per, 2)),
+            dma((layers // 2, per, 2)),
+            dma((chips, 2, 2)),
         ],
         compiler_params=pltpu.CompilerParams(
             collective_id=0, has_side_effects=True, vmem_limit_bytes=VMEM_LIMIT

time: 57.4 us -> 52.3 us (0.911)
  the two profiles are of different devices: /device:TPU:29 before, /device:TPU:3 now
where the time goes in v2:
time: 52.3 us; the launch traced here: 52.1 us
  Pallas kernels  50.2 us (96%)
  local copies, waits for them, and re-layouts  1.89 us (4%)
    pallas_call x1, Pallas kernels, scores(): pl.pallas_call(functools.partial(score_kernel, (dp, layers)), out_shape=j...  41.4 us
    pallas_call x1, Pallas kernels, precondition(): pl.pallas_call(precondition_kernel, out_shape=jax.ShapeDtypeStruct((count...  8.87 us
    unnamed x1, local copies, waits for them, and re-layouts  1.89 us

profile of v2, /device:TPU:3, one launch (start us, length us, event | category | flops | bytes accessed | tf_op | source)
XLA Modules:
  0.0 52.1 jit_solution(15214231172407022588)
XLA Ops:
  0.0 8.9 %precondition.1.p_ref = bf16[128,4096]{1,0:T(8,128)(2,1)} custom-call(bf16[128,4096]{1,0:T(8,128)(2,1)} %bitcast.6, f32[64,64]{1,0:T(8,128)} %bitcast.7, f32[64,64]{1,0:T(8,128)} %bitcast.8, f32[64,64]{1,0:T(8,128)} %bitcast.9), custom_call_target="tpu_custom_call" | custom-call | tf_op jit(solution)/shard_map/precondition/pallas_call | solution.py:108
  8.9 41.4 %scores.1 = f32[128,1024]{1,0:T(8,128)} custom-call(bf16[1024,4096]{1,0:T(8,128)(2,1)} %bitcast.5, bf16[128,4096]{1,0:T(8,128)(2,1)} %precondition.1.p_ref), custom_call_target="tpu_custom_call" | custom-call | tf_op jit(solution)/shard_map/scores/pallas_call | solution.py:385
  50.2 1.9 %copy.7 = f32[128,1024]{1,0:T(8,128)} copy(f32[128,1024]{1,0:T(8,128)} %scores.1) | data formatting | bytes 1048576

commit v3 on v2

--- a/solution.py
+++ b/solution.py
@@ -14,7 +14,7 @@
 VMEM_LIMIT = 56 * 1024 * 1024
 NT = (((1,), (1,)), ((), ()))
 D = 64
-CHUNK = 16
+CHUNKS = 8
 
 
 def dot_nt(a, b):
@@ -37,10 +37,10 @@
     return jnp.concatenate([high, high, low, low], axis=0)
 
 
-def precondition_kernel(
-    g_ref, bo_ref, bi_ref, s_ref, p_ref, wide, tall, square, rot, back, bo4, bi4, d4, w_in
+def precondition_rows(
+    g_ref, bo_ref, bi_ref, s_ref, scratch, put, finished
 ):
-    count = g_ref.shape[0]
+    wide, tall, square, rot, back, bo4, bi4, d4, w_in = scratch
     bo, bi = bo_ref[...], bi_ref[...]
     inverse = 1.0 / (s_ref[...] + damping)
 
@@ -99,37 +99,18 @@
             for i in range(2)
         ]
         block = jnp.transpose(jnp.concatenate(halves, axis=0))
-        p_ref[:, pair * 2 * D : (pair + 1) * 2 * D] = block.astype(bf16)
-
-
-def precondition(grads, bo, bi, s):
-    count, entries = grads.shape
-    vmem = pl.BlockSpec(memory_space=pltpu.VMEM)
-    return pl.pallas_call(
-        precondition_kernel,
-        out_shape=jax.ShapeDtypeStruct((count, entries), bf16),
-        in_specs=[vmem] * 4,
-        out_specs=vmem,
-        scratch_shapes=[
-            pltpu.VMEM((4 * D, 4 * D), f32),
-            pltpu.VMEM((4 * D, 2 * D), f32),
-            pltpu.VMEM((2 * D, 2 * D), f32),
-            pltpu.VMEM((entries, count), f32),
-            pltpu.VMEM((entries, count), f32),
-            pltpu.VMEM((D, 4 * D), f32),
-            pltpu.VMEM((D, 4 * D), f32),
-            pltpu.VMEM((2 * D, 4 * D), f32),
-            pltpu.VMEM((2 * D, 4 * D), bf16),
-        ],
-        compiler_params=pltpu.CompilerParams(vmem_limit_bytes=VMEM_LIMIT),
-        name="precondition",
-    )(grads, bo, bi, s)
+        put(pair * 2 * D, block.astype(bf16))
+        if (pair + 1) % (D // 2 // CHUNKS) == 0:
+            finished((pair + 1) // (D // 2 // CHUNKS) - 1)
 
 
 def score_kernel(
     sizes,
     train_hbm,
-    p_ref,
+    g_ref,
+    bo_ref,
+    bi_ref,
+    s_ref,
     out_ref,
     train,
     every,
@@ -147,12 +128,13 @@
     sum_send,
     sum_recv,
     relay_recv,
+    *scratch,
 ):
     dp, layers = sizes
     chips = dp // 2
     per = dp // layers
-    half = p_ref.shape[0] // 2
-    chunks = half // CHUNK
+    half = g_ref.shape[0] // 2
+    width = g_ref.shape[1] // CHUNKS
     n = train.shape[0]
     y = lax.axis_index("groups")
     me = lax.axis_index("dp")
@@ -171,54 +153,38 @@
     others = [sibling, across] + far + owners
     for other in others:
         pl.semaphore_signal(barrier, inc=1, device_id=other, device_id_type=MESH)
-    pl.semaphore_wait(barrier, len(others))
-
-    def rows(chunk):
-        return pl.ds(chunk * CHUNK, CHUNK)
 
     started = []
-    for chunk in range(chunks):
-        for o in range(1, chips):
-            source = p_ref.at[
-                pl.ds(pl.multiple_of(y * half + chunk * CHUNK, CHUNK), CHUNK), :
-            ]
-            started.append(
-                pltpu.make_async_remote_copy(
-                    source,
-                    every.at[x, y, core, rows(chunk), :],
-                    far_send.at[o, chunk],
-                    far_recv.at[o, chunk],
-                    device_id=far[o - 1],
-                    device_id_type=MESH,
-                )
-            )
-            started[-1].start()
-    for h in range(2):
+
+    def part(chip, h, c, chunk):
+        return every.at[chip, h, c, :, pl.ds(chunk * width, width)]
+
+    def send(chip, h, chunk, send_sem, recv_sem, to):
+        block = part(chip, h, core, chunk)
         copy = pltpu.make_async_remote_copy(
-            p_ref.at[pl.ds(h * half, half), :],
-            every.at[x, h, core],
-            core_send.at[0, h, 0],
-            core_recv.at[0, h, 0],
-            device_id=sibling,
-            device_id_type=MESH,
+            block, block, send_sem, recv_sem, device_id=to, device_id_type=MESH
         )
         copy.start()
         started.append(copy)
-    for h in range(2):
-        every[x, h, core] = p_ref[pl.ds(h * half, half), :]
+
+    def put(first, block):
+        for h in range(2):
+            every[x, h, core, :, first : first + 2 * D] = block[h * half : (h + 1) * half, :]
+
+    def finished(chunk):
+        if chunk == 0:
+            pl.semaphore_wait(barrier, len(others))
+        for o in range(1, chips):
+            send(x, y, chunk, far_send.at[o, chunk], far_recv.at[o, chunk], far[o - 1])
+        for h in range(2):
+            send(x, h, chunk, core_send.at[0, h, chunk], core_recv.at[0, h, chunk], sibling)
+
+    precondition_rows(g_ref, bo_ref, bi_ref, s_ref, scratch, put, finished)
 
     def arrived(ref, sem):
         pltpu.make_async_remote_copy(
             ref, ref, sem, sem, device_id=sibling, device_id_type=MESH
         ).wait_recv()
-
-    def forward(chip, h, chunk, send, recv, to):
-        block = every.at[chip, h, core, rows(chunk), :]
-        copy = pltpu.make_async_remote_copy(
-            block, block, send, recv, device_id=to, device_id_type=MESH
-        )
-        copy.start()
-        started.append(copy)
 
     partner = z + 1 - 2 * (z % 2)
 
@@ -277,74 +243,78 @@
 
     tile = min(n, 256)
 
-    def score_tile(chip, hs, t):
-        columns = pl.ds(pl.multiple_of(t * tile, tile), tile)
-        left = every[chip] if len(hs) == 2 else every[chip, hs[0]]
-        product = dot_nt(left.reshape(-1, every.shape[-1]), train[columns, :])
-        for i, h in enumerate(hs):
-            for c in range(2):
-                first = (i * 2 + c) * half
-                piece = product[first : first + half, :]
-                exact[chip, h, c, :, columns] = piece
-                ours[chip, h, c, :, columns] = piece.astype(bf16)
-
-    def score(chip, hs):
+    def score(chip, hs, chunk):
+        depth = pl.ds(chunk * width, width)
+
         def step(t, carry):
-            score_tile(chip, hs, t)
+            columns = pl.ds(pl.multiple_of(t * tile, tile), tile)
+            if len(hs) == 2:
+                left = every[chip, :, :, :, depth]
+            else:
+                left = every[chip, hs[0], :, :, depth]
+            product = dot_nt(left.reshape(-1, width), train[columns, depth])
+            for i, h in enumerate(hs):
+                for c in range(2):
+                    first = (i * 2 + c) * half
+                    piece = product[first : first + half, :]
+                    if chunk > 0:
+                        piece = piece + exact[chip, h, c, :, columns]
+                    exact[chip, h, c, :, columns] = piece
+                    if chunk == CHUNKS - 1:
+                        ours[chip, h, c, :, columns] = piece.astype(bf16)
             return carry
 
         lax.fori_loop(0, n // tile, step, 0)
-        send_sums(chip, hs)
-
-    for h in range(2):
-        arrived(every.at[x, h, 1 - core], core_recv.at[0, h, 0])
+        if chunk == CHUNKS - 1:
+            send_sums(chip, hs)
+
+    def pass_on(o, chunk):
+        source = (x + chips - o) % chips
+        arrived(part(source, y, core, chunk), far_recv.at[o, chunk])
+        send(source, y, chunk, row_send.at[o, chunk], row_recv.at[o, chunk], across)
+        send(source, y, chunk, core_send.at[o, 0, chunk], core_recv.at[o, 0, chunk], sibling)
+
     load.wait()
-    def pass_on(chunk):
-        for o in range(1, chips):
-            source = (x + chips - o) % chips
-            arrived(every.at[source, y, core, rows(chunk), :], far_recv.at[o, chunk])
-            forward(source, y, chunk, row_send.at[o, chunk], row_recv.at[o, chunk], across)
-            forward(
-                source, y, chunk, core_send.at[o, 0, chunk], core_recv.at[o, 0, chunk], sibling
-            )
-
     passed = 0
-    for t in range(n // tile):
-        score_tile(x, (0, 1), t)
-        if passed < chunks and t < n // tile - 1:
-            pass_on(passed)
+    for chunk in range(CHUNKS):
+        for h in range(2):
+            arrived(part(x, h, 1 - core, chunk), core_recv.at[0, h, chunk])
+        score(x, (0, 1), chunk)
+        if chunk % 2 == 1:
+            pass_on(1, passed)
             passed += 1
-    send_sums(x, (0, 1))
-    for chunk in range(passed, chunks):
-        pass_on(chunk)
     for o in range(1, chips):
         source = (x + chips - o) % chips
-        for chunk in range(chunks):
-            arrived(every.at[source, y, 1 - core, rows(chunk), :], core_recv.at[o, 0, chunk])
-        score(source, (y,))
+        for chunk in range(CHUNKS):
+            if o > 1 or chunk >= passed:
+                pass_on(o, chunk)
+            if chunk > 0:
+                arrived(part(source, y, 1 - core, chunk - 1), core_recv.at[o, 0, chunk - 1])
+                score(source, (y,), chunk - 1)
+        last = CHUNKS - 1
+        arrived(part(source, y, 1 - core, last), core_recv.at[o, 0, last])
+        score(source, (y,), last)
     pieces = [(h, c) for h in range(2) for c in range(2)]
     for o in range(1, chips):
         source = (x + chips - o) % chips
-        for chunk in range(chunks):
-            arrived(every.at[source, 1 - y, core, rows(chunk), :], row_recv.at[o, chunk])
-            forward(
-                source,
-                1 - y,
-                chunk,
-                core_send.at[o, 1, chunk],
-                core_recv.at[o, 1, chunk],
-                sibling,
-            )
-            if o == 1 and chunk < len(pieces):
-                combine(x, *pieces[chunk])
-        if o == 1:
-            for h, c in pieces[chunks:]:
-                combine(x, h, c)
-        for chunk in range(chunks):
-            arrived(
-                every.at[source, 1 - y, 1 - core, rows(chunk), :], core_recv.at[o, 1, chunk]
-            )
-        score(source, (1 - y,))
+        for chunk in range(CHUNKS + 1):
+            if chunk < CHUNKS:
+                arrived(part(source, 1 - y, core, chunk), row_recv.at[o, chunk])
+                send(
+                    source,
+                    1 - y,
+                    chunk,
+                    core_send.at[o, 1, chunk],
+                    core_recv.at[o, 1, chunk],
+                    sibling,
+                )
+            if chunk > 0:
+                arrived(
+                    part(source, 1 - y, 1 - core, chunk - 1), core_recv.at[o, 1, chunk - 1]
+                )
+                score(source, (1 - y,), chunk - 1)
+    for h, c in pieces:
+        combine(x, h, c)
     for o in range(1, chips):
         source = (x + chips - o) % chips
         for h in (y, 1 - y):
@@ -375,17 +345,17 @@
                 relay_copy(chip, h, c).wait_send()
 
 
-def scores(train_rows, ready, dp, layers):
+def scores(train_rows, grads, bo, bi, s, dp, layers):
     n, entries = train_rows.shape
-    count = ready.shape[0]
+    count = grads.shape[0]
     chips, per, half = dp // 2, dp // layers, count // 2
-    chunks = half // CHUNK
+    chunks = CHUNKS
     vmem = pl.BlockSpec(memory_space=pltpu.VMEM)
     dma = pltpu.SemaphoreType.DMA
     return pl.pallas_call(
         functools.partial(score_kernel, (dp, layers)),
         out_shape=jax.ShapeDtypeStruct((per * count, n), f32),
-        in_specs=[pl.BlockSpec(memory_space=pl.ANY), vmem],
+        in_specs=[pl.BlockSpec(memory_space=pl.ANY)] + [vmem] * 4,
         out_specs=vmem,
         scratch_shapes=[
             pltpu.VMEM((n, entries), bf16),
@@ -404,20 +374,36 @@
             dma((chips, 2, 2)),
             dma((layers // 2, per, 2)),
             dma((chips, 2, 2)),
+            pltpu.VMEM((4 * D, 4 * D), f32),
+            pltpu.VMEM((4 * D, 2 * D), f32),
+            pltpu.VMEM((2 * D, 2 * D), f32),
+            pltpu.VMEM((entries, count), f32),
+            pltpu.VMEM((entries, count), f32),
+            pltpu.VMEM((D, 4 * D), f32),
+            pltpu.VMEM((D, 4 * D), f32),
+            pltpu.VMEM((2 * D, 4 * D), f32),
+            pltpu.VMEM((2 * D, 4 * D), bf16),
         ],
         compiler_params=pltpu.CompilerParams(
             collective_id=0, has_side_effects=True, vmem_limit_bytes=VMEM_LIMIT
         ),
         name="scores",
-    )(train_rows, ready)
+    )(train_rows, grads, bo, bi, s)
 
 
 def solution(mesh):
     dp, layers = mesh.shape["dp"], mesh.shape["layer"]
 
     def body(train_grads, query_grads, basis_out, basis_in, scaling):
-        ready = precondition(query_grads[:, 0, :], basis_out[0], basis_in[0], scaling[0])
-        return scores(train_grads[:, 0, :], ready, dp, layers)
+        return scores(
+            train_grads[:, 0, :],
+            query_grads[:, 0, :],
+            basis_out[0],
+            basis_in[0],
+            scaling[0],
+            dp,
+            layers,
+        )
 
     in_specs = (
         P(("groups", "dp"), "layer", None),

time: 52.3 us -> 52.5 us (level)
  the two profiles are of different devices: /device:TPU:3 before, /device:TPU:0 now
where the time goes in v3:
time: 52.5 us; the launch traced here: 52.3 us
  Pallas kernels  50.4 us (96%)
  local copies, waits for them, and re-layouts  1.89 us (4%)
    pallas_call x1, Pallas kernels, scores(): pl.pallas_call(functools.partial(score_kernel, (dp, layers)), out_shape=j...  50.4 us
    unnamed x1, local copies, waits for them, and re-layouts  1.89 us

profile of v3, /device:TPU:0, one launch (start us, length us, event | category | flops | bytes accessed | tf_op | source)
XLA Modules:
  0.0 52.3 jit_solution(9576711418354630990)
XLA Ops:
  0.0 50.4 %scores.1 = f32[128,1024]{1,0:T(8,128)} custom-call(bf16[1024,4096]{1,0:T(8,128)(2,1)} %bitcast.5, bf16[128,4096]{1,0:T(8,128)(2,1)} %bitcast.6, f32[64,64]{1,0:T(8,128)} %bitcast.7, f32[64,64]{1,0:T(8,128)} %bitcast.8, f32[64,64]{1,0:T(8,128)} %bitcast.9), custom_call_target="tpu_custom_call" | custom-call | tf_op jit(solution)/shard_map/scores/pallas_call | solution.py:355
  50.5 1.9 %copy.7 = f32[128,1024]{1,0:T(8,128)} copy(f32[128,1024]{1,0:T(8,128)} %scores.1) | data formatting | bytes 1048576

commit v4 on v3

--- a/solution.py
+++ b/solution.py
@@ -243,30 +243,24 @@
 
     tile = min(n, 256)
 
-    def score(chip, hs, chunk):
-        depth = pl.ds(chunk * width, width)
-
+    def score_tile(chip, hs, t):
+        columns = pl.ds(pl.multiple_of(t * tile, tile), tile)
+        left = every[chip] if len(hs) == 2 else every[chip, hs[0]]
+        product = dot_nt(left.reshape(-1, every.shape[-1]), train[columns, :])
+        for i, h in enumerate(hs):
+            for c in range(2):
+                first = (i * 2 + c) * half
+                piece = product[first : first + half, :]
+                exact[chip, h, c, :, columns] = piece
+                ours[chip, h, c, :, columns] = piece.astype(bf16)
+
+    def score(chip, hs):
         def step(t, carry):
-            columns = pl.ds(pl.multiple_of(t * tile, tile), tile)
-            if len(hs) == 2:
-                left = every[chip, :, :, :, depth]
-            else:
-                left = every[chip, hs[0], :, :, depth]
-            product = dot_nt(left.reshape(-1, width), train[columns, depth])
-            for i, h in enumerate(hs):
-                for c in range(2):
-                    first = (i * 2 + c) * half
-                    piece = product[first : first + half, :]
-                    if chunk > 0:
-                        piece = piece + exact[chip, h, c, :, columns]
-                    exact[chip, h, c, :, columns] = piece
-                    if chunk == CHUNKS - 1:
-                        ours[chip, h, c, :, columns] = piece.astype(bf16)
+            score_tile(chip, hs, t)
             return carry
 
         lax.fori_loop(0, n // tile, step, 0)
-        if chunk == CHUNKS - 1:
-            send_sums(chip, hs)
+        send_sums(chip, hs)
 
     def pass_on(o, chunk):
         source = (x + chips - o) % chips
@@ -275,46 +269,41 @@
         send(source, y, chunk, core_send.at[o, 0, chunk], core_recv.at[o, 0, chunk], sibling)
 
     load.wait()
-    passed = 0
     for chunk in range(CHUNKS):
         for h in range(2):
             arrived(part(x, h, 1 - core, chunk), core_recv.at[0, h, chunk])
-        score(x, (0, 1), chunk)
-        if chunk % 2 == 1:
+    passed = 0
+    for t in range(n // tile):
+        score_tile(x, (0, 1), t)
+        while passed < min(CHUNKS, 2 * (t + 1)) and t < n // tile - 1:
             pass_on(1, passed)
             passed += 1
+    send_sums(x, (0, 1))
+    for o in range(1, chips):
+        source = (x + chips - o) % chips
+        for chunk in range(passed if o == 1 else 0, CHUNKS):
+            pass_on(o, chunk)
+        for chunk in range(CHUNKS):
+            arrived(part(source, y, 1 - core, chunk), core_recv.at[o, 0, chunk])
+        score(source, (y,))
+    pieces = [(h, c) for h in range(2) for c in range(2)]
     for o in range(1, chips):
         source = (x + chips - o) % chips
         for chunk in range(CHUNKS):
-            if o > 1 or chunk >= passed:
-                pass_on(o, chunk)
-            if chunk > 0:
-                arrived(part(source, y, 1 - core, chunk - 1), core_recv.at[o, 0, chunk - 1])
-                score(source, (y,), chunk - 1)
-        last = CHUNKS - 1
-        arrived(part(source, y, 1 - core, last), core_recv.at[o, 0, last])
-        score(source, (y,), last)
-    pieces = [(h, c) for h in range(2) for c in range(2)]
-    for o in range(1, chips):
-        source = (x + chips - o) % chips
-        for chunk in range(CHUNKS + 1):
-            if chunk < CHUNKS:
-                arrived(part(source, 1 - y, core, chunk), row_recv.at[o, chunk])
-                send(
-                    source,
-                    1 - y,
-                    chunk,
-                    core_send.at[o, 1, chunk],
-                    core_recv.at[o, 1, chunk],
-                    sibling,
-                )
-            if chunk > 0:
-                arrived(
-                    part(source, 1 - y, 1 - core, chunk - 1), core_recv.at[o, 1, chunk - 1]
-                )
-                score(source, (1 - y,), chunk - 1)
-    for h, c in pieces:
-        combine(x, h, c)
+            arrived(part(source, 1 - y, core, chunk), row_recv.at[o, chunk])
+            send(
+                source,
+                1 - y,
+                chunk,
+                core_send.at[o, 1, chunk],
+                core_recv.at[o, 1, chunk],
+                sibling,
+            )
+            if o == 1 and chunk % 2 == 1:
+                combine(x, *pieces[chunk // 2])
+        for chunk in range(CHUNKS):
+            arrived(part(source, 1 - y, 1 - core, chunk), core_recv.at[o, 1, chunk])
+        score(source, (1 - y,))
     for o in range(1, chips):
         source = (x + chips - o) % chips
         for h in (y, 1 - y):

time: 52.5 us -> 48.3 us (0.920)
  the two profiles are of different devices: /device:TPU:0 before, /device:TPU:10 now
where the time goes in v4:
time: 48.3 us; the launch traced here: 48.1 us
  Pallas kernels  46.2 us (96%)
  local copies, waits for them, and re-layouts  1.89 us (4%)
    pallas_call x1, Pallas kernels, scores(): pl.pallas_call(functools.partial(score_kernel, (dp, layers)), out_shape=j...  46.2 us
    unnamed x1, local copies, waits for them, and re-layouts  1.89 us

profile of v4, /device:TPU:10, one launch (start us, length us, event | category | flops | bytes accessed | tf_op | source)
XLA Modules:
  0.0 48.1 jit_solution(11694303036252804666)
XLA Ops:
  0.0 46.2 %scores.1 = f32[128,1024]{1,0:T(8,128)} custom-call(bf16[1024,4096]{1,0:T(8,128)(2,1)} %bitcast.5, bf16[128,4096]{1,0:T(8,128)(2,1)} %bitcast.6, f32[64,64]{1,0:T(8,128)} %bitcast.7, f32[64,64]{1,0:T(8,128)} %bitcast.8, f32[64,64]{1,0:T(8,128)} %bitcast.9), custom_call_target="tpu_custom_call" | custom-call | tf_op jit(solution)/shard_map/scores/pallas_call | solution.py:344
  46.2 1.9 %copy.7 = f32[128,1024]{1,0:T(8,128)} copy(f32[128,1024]{1,0:T(8,128)} %scores.1) | data formatting | bytes 1048576
